TPU v7x, 1024 devices: a whole 8x8x8 slice. The times are simulated.
1024 devices in a mesh: node: 8 (over y_lo, core), dp: 128 (over z, x, y_hi).
Axes of the slice: x: 8, y: 8 (y_hi: 2, y_lo: 4; y = y_hi * 4 + y_lo), z: 8, core: 2. Of those that a mesh axis runs over, the one named last changes fastest.
Arguments:
- activations: bfloat16 [131072, 4096], P(('node', 'dp')), may hold values from -24 to 24
- key_grads: bfloat16 [131072, 512], P(('node', 'dp')), may hold values from -6 to 6
- w_blocks: bfloat16 [4096, 512], P('node'), may hold values from -0.25 to 0.25
- w_scales: bfloat16 [32, 1], P('node'), may hold values from 0.5 to 2
- w_outliers: bfloat16 [64, 512], P('node'), may hold values from -1 to 1
- outlier_rows: int32 [32, 2], replicated, may hold values from 0 to 127, as said below
Outputs:
- input_grads: bfloat16 [131072, 4096], P(('node', 'dp'))
- weight_grad: float32 [4096, 512], P(('node', 'dp'))
Inputs may be any that keep to these rules, and one draw needn't show every extreme that they name: `outlier_rows`: the 2 entries of one block are distinct.
All inputs are finite; a program needn't handle non-finite values.
Results may differ from a plain program's by a relative error of at most 0.015.
Values may be sent and summed in bfloat16 or wider, within the bound.
A program may use at most 32 MiB of HBM per device.

v0:
```python
import jax
import jax.numpy as jnp
from jax import lax
from jax.sharding import PartitionSpec as P

D = 4096
BLOCK = 128
OUTL = 2
NB = 32


def outlier_mask(row_index):
    blocks_here = row_index.shape[0]
    positions = lax.broadcasted_iota(jnp.int32, (blocks_here, BLOCK), 1)
    marked = positions < 0
    for column in range(OUTL):
        marked = jnp.logical_or(marked, positions == row_index[:, column : column + 1])
    return marked


def dequantize(quantized, scales, outlier_vals, row_index):
    blocks_here = row_index.shape[0]
    width = quantized.shape[1]
    values = quantized.reshape(blocks_here, BLOCK, width).astype(jnp.float32) * scales.reshape(
        blocks_here, 1, 1
    ).astype(jnp.float32)
    extra = outlier_vals.reshape(blocks_here, OUTL, width).astype(jnp.float32)
    positions = lax.broadcasted_iota(jnp.int32, (blocks_here, BLOCK), 1)
    replacement = jnp.zeros((blocks_here, BLOCK, width), jnp.float32)
    for column in range(OUTL):
        chosen_rows = positions == row_index[:, column : column + 1]
        replacement = replacement + jnp.where(
            chosen_rows[:, :, None], extra[:, column : column + 1, :], 0.0
        )
    marked = outlier_mask(row_index)
    values = jnp.where(marked[:, :, None], replacement, values)
    return values.reshape(blocks_here * BLOCK, width).astype(jnp.bfloat16)


def on_device(activations, key_grads, w_blocks, w_scales, w_outliers, outlier_rows):
    rows_here = w_blocks.shape[0]
    blocks_here = rows_here // BLOCK
    width = w_blocks.shape[1]
    first_block = lax.axis_index("node") * blocks_here
    own_index = lax.dynamic_slice_in_dim(outlier_rows, first_block, blocks_here, 0)
    own_weight = dequantize(w_blocks, w_scales, w_outliers, own_index)
    pieces = lax.dot_general(
        lax.all_gather(key_grads, "node", axis=0, tiled=True),
        own_weight,
        (((1,), (1,)), ((), ())),
        preferred_element_type=jnp.float32,
    ).astype(jnp.bfloat16)
    input_grads = lax.all_to_all(pieces, "node", split_axis=0, concat_axis=1, tiled=True)
    total_tokens = activations.shape[0] * lax.axis_size("node") * lax.axis_size("dp")
    loss_scale = 1.0 / jnp.sqrt(jnp.float32(total_tokens))
    marked_flat = outlier_mask(outlier_rows).reshape(D)
    term = (
        lax.dot_general(
            activations, key_grads, (((0,), (0,)), ((), ())), preferred_element_type=jnp.float32
        )
        * loss_scale
    )
    bulk_sum = lax.psum_scatter(
        jnp.where(marked_flat[:, None], 0.0, term).astype(jnp.bfloat16),
        "node",
        scatter_dimension=0,
        tiled=True,
    ).astype(jnp.float32)
    block_base = lax.broadcasted_iota(jnp.int32, (NB, OUTL), 0) * BLOCK
    flat_rows = (block_base + outlier_rows).reshape(NB * OUTL)
    outlier_columns = jnp.take(activations, flat_rows, axis=1)
    outlier_part = (
        lax.dot_general(
            outlier_columns, key_grads, (((0,), (0,)), ((), ())), preferred_element_type=jnp.float32
        )
        * loss_scale
    )
    outlier_sum = lax.psum_scatter(
        outlier_part.astype(jnp.bfloat16), "node", scatter_dimension=0, tiled=True
    ).astype(jnp.float32)
    merged = bulk_sum.reshape(blocks_here, BLOCK, width)
    extra = outlier_sum.reshape(blocks_here, OUTL, width)
    positions = lax.broadcasted_iota(jnp.int32, (blocks_here, BLOCK), 1)
    for column in range(OUTL):
        chosen_rows = positions == own_index[:, column : column + 1]
        merged = jnp.where(chosen_rows[:, :, None], extra[:, column : column + 1, :], merged)
    weight_grad = lax.psum_scatter(
        merged.reshape(rows_here, width), "dp", scatter_dimension=0, tiled=True
    )
    return (input_grads, weight_grad)


def solution(mesh):
    in_specs = (
        P(("node", "dp"), None),
        P(("node", "dp"), None),
        P("node", None),
        P("node", None),
        P("node", None),
        P(),
    )
    out_specs = (P(("node", "dp"), None), P(("node", "dp"), None))
    return jax.shard_map(
        on_device, mesh=mesh, in_specs=in_specs, out_specs=out_specs, check_vma=False
    )
```

profile of v0, /device:TPU:16, one launch (start us, length us, event | category | flops | bytes accessed | tf_op | source)
XLA Modules:
  0.0 1864.1 jit_solution(16872173600025793599)
XLA Ops:
  7.2 0.0 reduce-scatter.3.cloned.1.call-start
  7.2 0.7 broadcast_add_fusion
  7.9 0.1 copy.17
  8.0 0.1 reshape.190
  8.1 0.1 reshape.189
  8.2 1.6 copy.19
  9.9 0.6 gather_fusion
  10.5 1.7 fusion.1
  12.2 0.0 reduce-scatter.3.cloned.1.call-update
  12.3 0.0 reduce-scatter.5.cloned.1.call-start
  12.3 0.8 slice_bitcast_fusion.1
  13.1 0.1 fusion.9
  13.2 4.0 select_convert_fusion
  17.1 0.0 copy-start.1
  17.1 0.0 copy-start.2
  17.1 0.0 copy-start.3
  17.1 0.0 copy-start
  17.1 0.0 reduce-scatter.5.cloned.1.call-update
  17.2 0.0 all-gather.2.cloned.1.call-start
  17.2 0.7 all-gather.2.cloned.1.call-update
  17.9 0.0 copy-done.1
  17.9 0.1 constant_dynamic-slice_fusion.1
  18.0 0.0 copy-done.2
  18.0 0.0 copy-done.3
  18.0 0.1 broadcast_bitcast_fusion
  18.1 0.1 fusion.15
  18.2 42.4 %reduce-scatter.3.cloned.1.call-done = bf16[8,512]{1,0:T(8,128)(2,1)} async-done(((bf16[64,512]{1,0:T(8,128)(2,1)}), bf16[8,512]{1,0:T(8,128)(2,1)}) %reduce-scatter.3.cloned.1.call-update) | async-done | bytes 8208 | tf_op jit(solution)/shard_map/reduce_scatter | solution.py:78
  60.6 0.7 reshape.196
  61.3 61.9 %reduce-scatter.5.cloned.1.call-done = bf16[512,512]{1,0:T(8,128)(2,1)} async-done(((bf16[4096,512]{1,0:T(8,128)(2,1)}), bf16[512,512]{1,0:T(8,128)(2,1)}) %reduce-scatter.5.cloned.1.call-update) | async-done | bytes 524304 | tf_op jit(solution)/shard_map/reduce_scatter | solution.py:63
  123.3 0.0 copy-done
  123.3 2.4 fusion.2
  125.7 43.9 %all-gather.2.cloned.1.call-done = bf16[1024,512]{1,0:T(8,128)(2,1)} async-done(((bf16[128,512]{1,0:T(8,128)(2,1)}), bf16[1024,512]{1,0:T(8,128)(2,1)}) %all-gather.2.cloned.1.call-update) | async-done | bytes 1048592 | tf_op jit(solution)/shard_map/all_gather | solution.py:48
  169.6 2.0 fusion
  171.5 1.2 copy.31
  172.7 7.9 all-to-all-start
  180.6 0.0 all-reduce.3.cloned.1.call-start
  180.6 0.6 all-reduce.3.cloned.1.call-update
  181.2 1.3 dynamic-slice
  183.1 1671.8 %all-reduce.3.cloned.1.call-done = f32[512,512]{1,0:T(8,128)} async-done(((f32[512,512]{1,0:T(8,128)}), f32[512,512]{1,0:T(8,128)}) %all-reduce.3.cloned.1.call-update) | async-done | bytes 1048592
  1855.0 1.3 constant_dynamic-slice_fusion
  1856.3 0.0 all-to-all-done
  1856.3 1.3 copy.20
  (11 shorter events, 0.1 us)
Async XLA Ops:
  7.2 53.4 %reduce-scatter.3.cloned.1.call-start = ((), (), s32[]{:S(2)}) async-start(), calls=%async_computation.4 | async-start | bytes 73728 | tf_op jit(solution)/shard_map/reduce_scatter | solution.py:78
  12.3 111.0 %reduce-scatter.5.cloned.1.call-start = ((), (), s32[]{:S(2)}) async-start(), calls=%async_computation.5 | async-start | bytes 4718592 | tf_op jit(solution)/shard_map/reduce_scatter | solution.py:63
  17.1 0.8 copy-start.1
  17.1 0.9 copy-start.2
  17.1 0.9 copy-start.3
  17.1 106.1 %copy-start = (bf16[512,512]{1,0:T(8,128)(2,1)S(1)}, bf16[512,512]{1,0:T(8,128)(2,1)}, u32[]{:S(2)}) copy-start(bf16[512,512]{1,0:T(8,128)(2,1)} %param.8) | copy-start | bytes 1572868
  17.2 152.4 %all-gather.2.cloned.1.call-start = ((), (), s32[]{:S(2)}) async-start(), calls=%async_computation.3 | async-start | bytes 1179648 | tf_op jit(solution)/shard_map/all_gather | solution.py:48
  172.7 1683.6 %all-to-all-start = ((bf16[8,128,512]{1,2,0:T(8,128)(2,1)}), bf16[8,128,512]{1,2,0:T(8,128)(2,1)S(1)}, u32[]{:S(2)}, u32[]{:S(2)}) async-start(bf16[8,128,512]{1,2,0:T(8,128)(2,1)} %bitcast.63), calls=%async_computation | async-start | bytes 2097152 | tf_op jit(solution)/shard_map/all_to_all | solution.py:53
  180.6 1674.3 %all-reduce.3.cloned.1.call-start = ((), (), s32[]{:S(2)}) async-start(), calls=%async_computation.6 | async-start | bytes 2097152
Sparse Core Ops, SparseCore 0:
  12.4 48.1 reduce-scatter.2
  64.4 58.8 reduce-scatter.4
  126.3 43.2 all-gather.1
  185.6 1669.3 all-reduce.2
where the time goes:
time: 1860 us
  waiting for transfers between devices  1820 us (98%)
    unnamed x5, waiting for transfers between devices  1670 us
    reduce_scatter x1, waiting for transfers between devices, on_device(): lax.psum_scatter(jnp.where(marked_flat[:, None], 0.0, term).astype(jnp.bf...  61.9 us
    all_gather x1, waiting for transfers between devices, on_device(): lax.all_gather(key_grads, 'node', axis=0, tiled=True)  43.9 us
    reduce_scatter x1, waiting for transfers between devices, on_device(): lax.psum_scatter(outlier_part.astype(jnp.bfloat16), 'node', scatter_dimen...  42.4 us
  transfers between devices with their start and end apart: 5, of which 4 were waited for; matrix products, arithmetic and copies ran while one was open for 1% of the time, Pallas kernels for 0%

commit v1 on v0

v1 whole, which is shorter than its diff:
```python
import jax
import jax.numpy as jnp
from jax import lax
from jax.experimental import pallas as pl
from jax.experimental.pallas import tpu as pltpu
from jax.sharding import PartitionSpec as P

D = 4096
KW = 512
BLOCK = 128
TOK = 128
TOKENS = 131072
RING = 8
YLO = 4
MESH = pl.DeviceIdType.MESH


def kernel(
    act, key, wq, scales, wout, rows,
    ig, wg,
    a_all, k_all, w_raw, w_all, part0, part1, ring_in, s2_in, s3_out, s3_in, ig_own, ig_sib,
    loc_sem, ex_send, ex_recv, w_send, w_recv, ring_send, ring_recv,
    s2_send, s2_recv, s3_send, s3_recv, ig_loc, ig_send, ig_recv,
):
    node, dp = lax.axis_index("node"), lax.axis_index("dp")
    core, ylo = node % 2, node // 2
    z, x, yhi = dp // 16, (dp // 2) % 8, dp % 2
    y = yhi * 4 + ylo
    part = (part0, part1)
    place = (x, z)

    def at(px, py, pz, pc):
        return ((py % 4) * 2 + pc, pz * 16 + px * 2 + py // 4)

    def on_x(step):
        return at((x + step) % RING, y, z, core)

    def on_y(step):
        return at(x, (y + step) % RING, z, core)

    def on_z(step):
        return at(x, y, (z + step) % RING, core)

    sibling = at(x, y, z, 1 - core)
    first_axis = (on_x, on_z)
    second_axis = (on_z, on_x)

    def columns(block, whose):
        return pl.ds(pl.multiple_of((2 * block + whose) * 512, 512), 512)

    def remote(src, dst, send, recv, device):
        return pltpu.make_async_remote_copy(
            src_ref=src, dst_ref=dst, send_sem=send, recv_sem=recv,
            device_id=device, device_id_type=MESH,
        )

    local_w = pltpu.make_async_copy(wq, w_raw, loc_sem.at[0])
    local_k = pltpu.make_async_copy(key, k_all.at[pl.ds(0, TOK)], loc_sem.at[1])
    local_a = [
        pltpu.make_async_copy(
            act.at[:, columns(b, core)],
            a_all.at[pl.ds(0, TOK), pl.ds(b * 512, 512)],
            loc_sem.at[2 + b],
        )
        for b in range(YLO)
    ]
    local_w.start()
    local_k.start()
    for copy in local_a:
        copy.start()

    barrier = pltpu.get_barrier_semaphore()
    pl.semaphore_signal(barrier, inc=1, device_id=sibling, device_id_type=MESH)
    for along in (on_x, on_y, on_z):
        for step in range(1, RING):
            pl.semaphore_signal(barrier, inc=1, device_id=along(step), device_id_type=MESH)

    local_w.wait()
    scale = scales[...].astype(jnp.float32)
    extra = wout[...].astype(jnp.float32)
    spot = lax.broadcasted_iota(jnp.int32, (BLOCK, KW), 0)
    for b in range(4):
        values = w_raw[pl.ds(b * BLOCK, BLOCK), :].astype(jnp.float32) * scale[:, b : b + 1]
        for j in range(2):
            row = rows[j, node * 4 + b]
            values = jnp.where(spot == row, extra[2 * b + j : 2 * b + j + 1, :], values)
        w_all[0, pl.ds(b * BLOCK, BLOCK), :] = values.astype(jnp.bfloat16)

    pl.semaphore_wait(barrier, 1 + 3 * (RING - 1))

    exchange = [remote(key, k_all.at[pl.ds(TOK, TOK)], ex_send.at[4], ex_recv.at[4], sibling)]
    for b in range(YLO):
        exchange.append(
            remote(
                act.at[:, columns(b, 1 - core)],
                a_all.at[pl.ds(TOK, TOK), pl.ds(b * 512, 512)],
                ex_send.at[b], ex_recv.at[b], sibling,
            )
        )
    for copy in exchange:
        copy.start()

    def half(slot, index):
        return w_all.at[slot, pl.ds(index * 256, 256)]

    weight = {}
    for direction, step in ((0, 1), (1, -1)):
        for order in range(2):
            index = order if direction == 0 else 1 - order
            copy = remote(
                half(0, index), half(1 + direction, index),
                w_send.at[direction, order], w_recv.at[direction, order], on_y(step),
            )
            copy.start()
            weight[direction, order] = copy

    def relay_weight():
        for direction, step in ((0, 1), (1, -1)):
            weight[direction, 0].wait_recv()
            copy = remote(
                half(1 + direction, direction), half(3, direction),
                w_send.at[direction, 2], w_recv.at[direction, 2], on_y(step),
            )
            copy.start()
            weight[direction, 2] = copy

    def piece(p, chunk, h):
        return part[p].at[chunk, pl.ds(2 * h, 2)]

    ring = {}

    def send_ring(p, direction, h, hop):
        sign = 1 if direction == 0 else -1
        chunk = (place[p] + sign * (4 - hop)) % RING
        if hop > (0 if h == direction else 1):
            ring[p, direction, h, hop - 1].wait_recv()
            total = part[p][chunk, pl.ds(2 * h, 2)].astype(jnp.float32) + ring_in[
                p, direction, h, hop - 1
            ].astype(jnp.float32)
            part[p][chunk, pl.ds(2 * h, 2)] = total.astype(jnp.bfloat16)
        copy = remote(
            piece(p, chunk, h), ring_in.at[p, direction, h, hop],
            ring_send.at[p, direction, h, hop], ring_recv.at[p, direction, h, hop],
            first_axis[p](sign),
        )
        copy.start()
        ring[p, direction, h, hop] = copy

    def partial(b):
        local_a[b].wait()
        exchange[1 + b].wait_recv()
        product = lax.dot_general(
            a_all[:, pl.ds(b * 512, 512)], k_all[...], (((0,), (0,)), ((), ())),
            preferred_element_type=jnp.float32,
        )
        for p in range(2):
            tiles = [
                product[:, (2 * p + c) * 128 : (2 * p + c + 1) * 128].reshape(8, 8, 8, 128)
                for c in range(2)
            ]
            both = jnp.concatenate(tiles, axis=2).astype(jnp.bfloat16)
            for i in range(8):
                part[p][i, b] = both[:, i] if p == 0 else both[i]

    local_k.wait()
    exchange[0].wait_recv()
    for h in range(2):
        partial(2 * h)
        partial(2 * h + 1)
        for p in range(2):
            send_ring(p, h, h, 0)
        for p in range(2):
            send_ring(p, 1 - h, h, 1)

    grads = {}

    def input_grads(slot, away):
        out = lax.dot_general(
            k_all[...], w_all[slot], (((1,), (1,)), ((), ())), preferred_element_type=jnp.float32
        ).astype(jnp.bfloat16)
        ig_own[slot] = out[:TOK]
        ig_sib[slot] = out[TOK:]
        where = columns((ylo + away) % YLO, core)
        local = pltpu.make_async_copy(ig_own.at[slot], ig.at[:, where], ig_loc.at[slot])
        local.start()
        copy = remote(
            ig_sib.at[slot], ig.at[:, where], ig_send.at[slot], ig_recv.at[slot], sibling
        )
        copy.start()
        grads[slot] = (local, copy)

    input_grads(0, 0)
    for p in range(2):
        for direction in range(2):
            send_ring(p, direction, direction, 1)
    for p in range(2):
        for direction in range(2):
            send_ring(p, direction, 1 - direction, 2)
    relay_weight()
    for p in range(2):
        for direction in range(2):
            send_ring(p, direction, direction, 2)
    for p in range(2):
        for direction in range(2):
            send_ring(p, direction, 1 - direction, 3)
    for p in range(2):
        for direction in range(2):
            send_ring(p, direction, direction, 3)
    for direction, away in ((0, -1), (1, 1)):
        weight[direction, 1].wait_recv()
        input_grads(1 + direction, away)

    other = (z, x)
    second = {}
    for p in range(2):
        for h in range(2):
            total = part[p][place[p], pl.ds(2 * h, 2)].astype(jnp.float32)
            for direction in range(2):
                ring[p, direction, h, 3].wait_recv()
                total = total + ring_in[p, direction, h, 3].astype(jnp.float32)
            part[p][place[p], pl.ds(2 * h, 2)] = total.astype(jnp.bfloat16)
        for step in (4, 3, 5, 2, 6, 1, 7):
            copy = remote(
                part[p].at[place[p], :, (other[p] + step) % RING], s2_in.at[p, step],
                s2_send.at[p, step], s2_recv.at[p, step], second_axis[p](step),
            )
            copy.start()
            second[p, step] = copy

    for direction in range(2):
        weight[direction, 2].wait_recv()
    input_grads(3, 2)

    for p in range(2):
        total = part[p][place[p], :, other[p]].astype(jnp.float32)
        for step in (1, 7, 2, 6, 3, 5, 4):
            second[p, step].wait_recv()
            total = total + s2_in[p, step].astype(jnp.float32)
        s3_out[:, p] = total.astype(jnp.bfloat16)
    third = {}
    for step in (4, 3, 5, 2, 6, 1, 7):
        copy = remote(
            s3_out.at[(ylo + step) % YLO], s3_in.at[step], s3_send.at[step], s3_recv.at[step],
            on_y(step),
        )
        copy.start()
        third[step] = copy
    total = s3_out[ylo].astype(jnp.float32)
    for step in (1, 7, 2, 6, 3, 5, 4):
        third[step].wait_recv()
        total = total + s3_in[step].astype(jnp.float32)
    total = total * (1.0 / TOKENS ** 0.5)
    for p in range(2):
        for c in range(2):
            low, high = total[p, 8 * c : 8 * c + 4], total[p, 8 * c + 4 : 8 * c + 8]
            wg[:, (2 * p + c) * 128 : (2 * p + c + 1) * 128] = jnp.where(yhi == 0, low, high)

    for local, copy in grads.values():
        local.wait()
        copy.wait()
    for copy in exchange:
        copy.wait_send()
    for group in (weight, ring, second, third):
        for copy in group.values():
            copy.wait_send()


def on_device(activations, key_grads, w_blocks, w_scales, w_outliers, outlier_rows):
    bf16, dma = jnp.bfloat16, pltpu.SemaphoreType.DMA
    hbm, vmem = pl.BlockSpec(memory_space=pl.ANY), pl.BlockSpec(memory_space=pltpu.VMEM)
    return pl.pallas_call(
        kernel,
        out_shape=(
            jax.ShapeDtypeStruct((TOK, D), bf16),
            jax.ShapeDtypeStruct((4, KW), jnp.float32),
        ),
        in_specs=[hbm, hbm, hbm, vmem, vmem, pl.BlockSpec(memory_space=pltpu.SMEM)],
        out_specs=(hbm, vmem),
        scratch_shapes=[
            pltpu.VMEM((2 * TOK, D // 2), bf16),
            pltpu.VMEM((2 * TOK, KW), bf16),
            pltpu.VMEM((512, KW), bf16),
            pltpu.VMEM((4, 512, KW), bf16),
            pltpu.VMEM((8, YLO, 8, 16, 128), bf16),
            pltpu.VMEM((8, YLO, 8, 16, 128), bf16),
            pltpu.VMEM((2, 2, 2, 4, 2, 8, 16, 128), bf16),
            pltpu.VMEM((2, 8, YLO, 16, 128), bf16),
            pltpu.VMEM((YLO, 2, 16, 128), bf16),
            pltpu.VMEM((8, 2, 16, 128), bf16),
            pltpu.VMEM((4, TOK, 512), bf16),
            pltpu.VMEM((4, TOK, 512), bf16),
            dma((6,)), dma((5,)), dma((5,)), dma((2, 3)), dma((2, 3)),
            dma((2, 2, 2, 4)), dma((2, 2, 2, 4)),
            dma((2, 8)), dma((2, 8)), dma((8,)), dma((8,)), dma((4,)), dma((4,)), dma((4,)),
        ],
        compiler_params=pltpu.CompilerParams(
            collective_id=0, has_side_effects=True, vmem_limit_bytes=40 * 1024 * 1024
        ),
        cost_estimate=pl.CostEstimate(
            flops=4 * TOK * D * KW, bytes_accessed=4 * 1024 * 1024, transcendentals=0
        ),
    )(
        activations, key_grads, w_blocks, w_scales.reshape(1, -1), w_outliers, outlier_rows.T
    )


def solution(mesh):
    both = P(("node", "dp"), None)
    return jax.shard_map(
        on_device,
        mesh=mesh,
        in_specs=(both, both, P("node", None), P("node", None), P("node", None), P()),
        out_specs=(both, both),
        check_vma=False,
    )
```

time: 1860 us -> 62.2 us (0.03)
  the two profiles are of different devices: /device:TPU:16 before, /device:TPU:2 now
where the time goes in v1:
time: 62.2 us; the launch traced here: 61.9 us
  Pallas kernels  55.1 us (89%)
  local copies, waits for them, and re-layouts  6.1 us (10%)
  between operations  0.66 us (1%)
    pallas_call x1, Pallas kernels, on_device(): pl.pallas_call(kernel, out_shape=(jax.ShapeDtypeStruct((TOK, D), bf16), j...  55.1 us
    unnamed x14, local copies, waits for them, and re-layouts  6.1 us

profile of v1, /device:TPU:2, one launch (start us, length us, event | category | flops | bytes accessed | tf_op | source)
XLA Modules:
  0.0 61.9 jit_solution(8059732218301992417)
XLA Ops:
  0.6 0.0 copy-start.4
  0.6 0.0 copy-start.5
  0.7 0.7 %copy-done.4 = s32[32,2]{0,1:T(2,128)S(1)} copy-done((s32[32,2]{0,1:T(2,128)S(1)}, s32[32,2]{0,1:T(2,128)}, u32[]{:S(2)}) %copy-start.4) | copy-done | bytes 280
  1.3 0.0 copy-done.5
  1.3 0.0 copy-start
  1.3 1.2 %copy-done = bf16[128,4096]{1,0:T(8,128)(2,1)S(1)} copy-done((bf16[128,4096]{1,0:T(8,128)(2,1)S(1)}, bf16[128,4096]{1,0:T(8,128)(2,1)}, u32[]{:S(2)}) %copy-start) | copy-done | bytes 1048600
  2.5 0.0 copy-start.1
  2.5 1.0 %copy-done.1 = bf16[512,512]{1,0:T(8,128)(2,1)S(1)} copy-done((bf16[512,512]{1,0:T(8,128)(2,1)S(1)}, bf16[512,512]{1,0:T(8,128)(2,1)}, u32[]{:S(2)}) %copy-start.1) | copy-done | bytes 524312
  3.6 0.0 copy-start.2
  3.6 0.9 %copy-done.2 = bf16[128,512]{1,0:T(8,128)(2,1)S(1)} copy-done((bf16[128,512]{1,0:T(8,128)(2,1)S(1)}, bf16[128,512]{1,0:T(8,128)(2,1)}, u32[]{:S(2)}) %copy-start.2) | copy-done | bytes 131096
  4.5 0.0 copy-start.3
  4.5 0.7 %copy-done.3 = bf16[8,512]{1,0:T(8,128)(2,1)S(1)} copy-done((bf16[8,512]{1,0:T(8,128)(2,1)S(1)}, bf16[8,512]{1,0:T(8,128)(2,1)}, u32[]{:S(2)}) %copy-start.3) | copy-done | bytes 8216
  5.2 55.1 %shard_map.77 = (bf16[128,4096]{1,0:T(8,128)(2,1)S(1)}, f32[4,512]{1,0:T(4,128)S(1)}) custom-call(bf16[128,4096]{1,0:T(8,128)(2,1)S(1)} %copy-done, bf16[128,512]{1,0:T(8,128)(2,1)S(1)} %copy-done.2, bf16[512,512]{1,0:T(8,128)(2,1)S(1)} %copy-done.1, bf16[1,4]{1,0:T(2,128)(2,1)S(1)} %bitcast.3, bf16[8,512]{1,0:T(8,128)(2,1)S(1)} %copy-done.3, ...), custom_call_target="tpu_custom_call" | custom-call | flops 1073741824 | bytes 4194304 | tf_op jit(solution)/shard_map/pallas_call | solution.py:271
  60.3 1.0 %copy.10 = bf16[128,4096]{1,0:T(8,128)(2,1)} copy(bf16[128,4096]{1,0:T(8,128)(2,1)S(1)} %get-tuple-element.4) | data formatting | bytes 2097152
  61.3 0.6 copy.11
Async XLA Ops:
  0.6 0.7 %copy-start.4 = (s32[32,2]{0,1:T(2,128)S(1)}, s32[32,2]{0,1:T(2,128)}, u32[]{:S(2)}) copy-start(s32[32,2]{0,1:T(2,128)} %param.11) | copy-start | bytes 772
  0.6 0.7 %copy-start.5 = (bf16[4,1]{0,1:T(2,128)(2,1)S(1)}, bf16[4,1]{0,1:T(2,128)(2,1)}, u32[]{:S(2)}) copy-start(bf16[4,1]{0,1:T(2,128)(2,1)} %param.9) | copy-start | bytes 28
  1.3 1.2 %copy-start = (bf16[128,4096]{1,0:T(8,128)(2,1)S(1)}, bf16[128,4096]{1,0:T(8,128)(2,1)}, u32[]{:S(2)}) copy-start(bf16[128,4096]{1,0:T(8,128)(2,1)} %act.1) | copy-start | bytes 3145732
  2.5 1.0 %copy-start.1 = (bf16[512,512]{1,0:T(8,128)(2,1)S(1)}, bf16[512,512]{1,0:T(8,128)(2,1)}, u32[]{:S(2)}) copy-start(bf16[512,512]{1,0:T(8,128)(2,1)} %wq.1) | copy-start | bytes 1572868
  3.6 0.9 %copy-start.2 = (bf16[128,512]{1,0:T(8,128)(2,1)S(1)}, bf16[128,512]{1,0:T(8,128)(2,1)}, u32[]{:S(2)}) copy-start(bf16[128,512]{1,0:T(8,128)(2,1)} %key.1) | copy-start | bytes 393220
  4.5 0.7 %copy-start.3 = (bf16[8,512]{1,0:T(8,128)(2,1)S(1)}, bf16[8,512]{1,0:T(8,128)(2,1)}, u32[]{:S(2)}) copy-start(bf16[8,512]{1,0:T(8,128)(2,1)} %wout.1) | copy-start | bytes 24580

commit v2 on v1

v2 whole, which is shorter than its diff:
```python
import jax
import jax.numpy as jnp
from jax import lax
from jax.experimental import pallas as pl
from jax.experimental.pallas import tpu as pltpu
from jax.sharding import PartitionSpec as P

D = 4096
KW = 512
BLOCK = 128
TOK = 128
TOKENS = 131072
RING = 8
YLO = 4
VMEM_BYTES = 56 * 1024 * 1024
MESH = pl.DeviceIdType.MESH


def kernel(
    act, key, wq, scales_in, wout_in, rows_in,
    ig, wg,
    scales, wout, rows, a_all, k_all, w_raw, w_all, part0, part1, ring_in, s2_in, s3_out, s3_in, ig_own, ig_sib,
    loc_sem, ex_send, ex_recv, w_send, w_recv, ring_send, ring_recv,
    s2_send, s2_recv, s3_send, s3_recv, ig_loc, ig_send, ig_recv,
):
    node, dp = lax.axis_index("node"), lax.axis_index("dp")
    core, ylo = node % 2, node // 2
    z, x, yhi = dp // 16, (dp // 2) % 8, dp % 2
    y = yhi * 4 + ylo
    part = (part0, part1)
    place = (x, z)
    other = (z, x)

    def at(px, py, pz, pc):
        return ((py % 4) * 2 + pc, pz * 16 + px * 2 + py // 4)

    def on_x(step):
        return at((x + step) % RING, y, z, core)

    def on_y(step):
        return at(x, (y + step) % RING, z, core)

    def on_z(step):
        return at(x, y, (z + step) % RING, core)

    sibling = at(x, y, z, 1 - core)
    first_axis = (on_x, on_z)
    second_axis = (on_z, on_x)

    def columns(block, whose):
        return pl.ds(pl.multiple_of((2 * block + whose) * 512, 512), 512)

    def remote(src, dst, send, recv, device):
        return pltpu.make_async_remote_copy(
            src_ref=src, dst_ref=dst, send_sem=send, recv_sem=recv,
            device_id=device, device_id_type=MESH,
        )

    barrier = pltpu.get_barrier_semaphore()
    for step in (4, 3, 5, 2, 6, 1, 7):
        for along in (on_y, on_x, on_z):
            pl.semaphore_signal(barrier, inc=1, device_id=along(step), device_id_type=MESH)
    pl.semaphore_signal(barrier, inc=1, device_id=sibling, device_id_type=MESH)

    local_w = pltpu.make_async_copy(wq, w_raw, loc_sem.at[0])
    local_k = pltpu.make_async_copy(key, k_all.at[pl.ds(0, TOK)], loc_sem.at[1])
    local_a = [
        pltpu.make_async_copy(
            act.at[:, columns(b, core)],
            a_all.at[pl.ds(0, TOK), pl.ds(b * 512, 512)],
            loc_sem.at[2 + b],
        )
        for b in range(YLO)
    ]
    small = [
        pltpu.make_async_copy(src, dst, loc_sem.at[6 + i])
        for i, (src, dst) in enumerate(((scales_in, scales), (wout_in, wout), (rows_in, rows)))
    ]
    for copy in (*small, local_w, local_k, *local_a):
        copy.start()

    pl.semaphore_wait(barrier, 1 + 3 * (RING - 1))

    exchange = [remote(key, k_all.at[pl.ds(TOK, TOK)], ex_send.at[4], ex_recv.at[4], sibling)]
    for b in range(YLO):
        exchange.append(
            remote(
                act.at[:, columns(b, 1 - core)],
                a_all.at[pl.ds(TOK, TOK), pl.ds(b * 512, 512)],
                ex_send.at[b], ex_recv.at[b], sibling,
            )
        )
    for copy in exchange:
        copy.start()

    for copy in (*small, local_w):
        copy.wait()
    scale = scales[...].astype(jnp.float32)
    extra = wout[...].astype(jnp.float32)
    spot = lax.broadcasted_iota(jnp.int32, (BLOCK, KW), 0)
    for b in range(4):
        values = w_raw[pl.ds(b * BLOCK, BLOCK), :].astype(jnp.float32) * scale[:, b : b + 1]
        for j in range(2):
            row = rows[j, node * 4 + b]
            values = jnp.where(spot == row, extra[2 * b + j : 2 * b + j + 1, :], values)
        w_all[0, pl.ds(b * BLOCK, BLOCK), :] = values.astype(jnp.bfloat16)

    def half(slot, index):
        return w_all.at[slot, pl.ds(index * 256, 256)]

    weight = {}
    for direction, step in ((0, 1), (1, -1)):
        for order in range(2):
            index = order if direction == 0 else 1 - order
            copy = remote(
                half(0, index), half(1 + direction, index),
                w_send.at[direction, order], w_recv.at[direction, order], on_y(step),
            )
            copy.start()
            weight[direction, order] = copy

    def relay_weight():
        for direction, step in ((0, 1), (1, -1)):
            weight[direction, 0].wait_recv()
            copy = remote(
                half(1 + direction, direction), half(3, direction),
                w_send.at[direction, 2], w_recv.at[direction, 2], on_y(step),
            )
            copy.start()
            weight[direction, 2] = copy

    order = (0, 1, 3, 2)
    far_end = ((0, 3), (1, 2))

    def piece(p, chunk, s):
        return part[p].at[chunk, pl.ds(2 * s, 2)]

    ring = {}

    def send_ring(p, direction, s, hop):
        sign = 1 if direction == 0 else -1
        chunk = (place[p] + sign * (4 - hop)) % RING
        if hop > (0 if s in far_end[direction] else 1):
            ring[p, direction, s, hop - 1].wait_recv()
            part[p][chunk, pl.ds(2 * s, 2)] += ring_in[p, direction, s, hop - 1]
        copy = remote(
            piece(p, chunk, s), ring_in.at[p, direction, s, hop],
            ring_send.at[p, direction, s, hop], ring_recv.at[p, direction, s, hop],
            first_axis[p](sign),
        )
        copy.start()
        ring[p, direction, s, hop] = copy

    def round_of(far, hop):
        for s in order:
            for p in range(2):
                for direction in range(2):
                    if (s in far_end[direction]) == far:
                        send_ring(p, direction, s, hop)

    def partial(b):
        local_a[b].wait()
        exchange[1 + b].wait_recv()
        product = lax.dot_general(
            a_all[:, pl.ds(b * 512, 512)], k_all[...], (((0,), (0,)), ((), ())),
            preferred_element_type=jnp.float32,
        )
        for p in range(2):
            tiles = [
                product[:, (2 * p + c) * 128 : (2 * p + c + 1) * 128].reshape(8, 8, 8, 128)
                for c in range(2)
            ]
            both = jnp.concatenate(tiles, axis=2).astype(jnp.bfloat16)
            for i in range(8):
                slot = (i - other[p] + 5) % RING
                part[p][:, slot, b] = both[i] if p == 0 else both[:, i]

    local_k.wait()
    exchange[0].wait_recv()
    for b in range(YLO):
        partial(b)
    round_of(True, 0)
    round_of(False, 1)

    grads = {}

    def input_grads(slot, away):
        out = lax.dot_general(
            k_all[...], w_all[slot], (((1,), (1,)), ((), ())), preferred_element_type=jnp.float32
        ).astype(jnp.bfloat16)
        ig_own[slot] = out[:TOK]
        ig_sib[slot] = out[TOK:]
        where = columns((ylo + away) % YLO, core)
        local = pltpu.make_async_copy(ig_own.at[slot], ig.at[:, where], ig_loc.at[slot])
        local.start()
        copy = remote(
            ig_sib.at[slot], ig.at[:, where], ig_send.at[slot], ig_recv.at[slot], sibling
        )
        copy.start()
        grads[slot] = (local, copy)

    input_grads(0, 0)
    round_of(True, 1)
    round_of(False, 2)
    relay_weight()
    round_of(True, 2)
    round_of(False, 3)
    round_of(True, 3)

    second = {}
    for s in order:
        for p in range(2):
            total = part[p][place[p], pl.ds(2 * s, 2)].astype(jnp.float32)
            for direction in range(2):
                ring[p, direction, s, 3].wait_recv()
                total = total + ring_in[p, direction, s, 3].astype(jnp.float32)
            part[p][place[p], pl.ds(2 * s, 2)] = total.astype(jnp.bfloat16)
            for slot in (2 * s, 2 * s + 1):
                step = (slot + 3) % RING
                if step == 0:
                    continue
                copy = remote(
                    part[p].at[place[p], slot], s2_in.at[p, step],
                    s2_send.at[p, step], s2_recv.at[p, step], second_axis[p](step),
                )
                copy.start()
                second[p, step] = copy

    for direction, away in ((0, -1), (1, 1)):
        weight[direction, 1].wait_recv()
        input_grads(1 + direction, away)

    quads = [[], []]
    for p in range(2):
        total = part[p][place[p], 5].astype(jnp.float32)
        for step in (4, 3, 5, 2, 6, 1, 7):
            second[p, step].wait_recv()
            total = total + s2_in[p, step].astype(jnp.float32)
        for c in range(2):
            for upper in range(2):
                first = 8 * c + 4 * upper
                quads[upper].append(total[:, first : first + 4])
    for upper in range(2):
        rows_of = jnp.concatenate(quads[upper], axis=1)
        s3_out[pl.ds(YLO * upper, YLO)] = rows_of.astype(jnp.bfloat16)
    third = {}
    for step in (4, 3, 5, 2, 6, 1, 7):
        copy = remote(
            s3_out.at[(y + step) % RING], s3_in.at[step], s3_send.at[step], s3_recv.at[step],
            on_y(step),
        )
        copy.start()
        third[step] = copy
    for direction in range(2):
        weight[direction, 2].wait_recv()
    input_grads(3, 2)
    total = s3_out[y].astype(jnp.float32)
    for step in (1, 7, 2, 6, 3, 5, 4):
        third[step].wait_recv()
        total = total + s3_in[step].astype(jnp.float32)
    total = total * (1.0 / TOKENS ** 0.5)
    for c in range(4):
        wg[:, c * 128 : (c + 1) * 128] = total[4 * c : 4 * c + 4]

    for local, copy in grads.values():
        local.wait()
        copy.wait()
    for copy in exchange:
        copy.wait_send()
    for group in (weight, ring, second, third):
        for copy in group.values():
            copy.wait_send()


def hand_on(ig_in, wg_in, ig, wg, ig_buf, wg_buf, in_sems, out_sems):
    pieces = [(wg_in, wg_buf, wg)]
    for i in range(8):
        piece = pl.ds(i * 16, 16)
        pieces.append((ig_in.at[piece], ig_buf.at[piece], ig.at[piece]))
    loads = [pltpu.make_async_copy(p[0], p[1], in_sems.at[i]) for i, p in enumerate(pieces)]
    stores = [pltpu.make_async_copy(p[1], p[2], out_sems.at[i]) for i, p in enumerate(pieces)]
    for load in loads:
        load.start()
    for load, store in zip(loads, stores):
        load.wait()
        store.start()
    for store in stores:
        store.wait()


def on_device(activations, key_grads, w_blocks, w_scales, w_outliers, outlier_rows):
    bf16, dma = jnp.bfloat16, pltpu.SemaphoreType.DMA
    hbm, vmem = pl.BlockSpec(memory_space=pl.ANY), pl.BlockSpec(memory_space=pltpu.VMEM)
    shapes = (
        jax.ShapeDtypeStruct((TOK, D), bf16),
        jax.ShapeDtypeStruct((4, KW), jnp.float32),
    )
    results = pl.pallas_call(
        kernel,
        out_shape=shapes,
        in_specs=[hbm] * 6,
        out_specs=(hbm, vmem),
        scratch_shapes=[
            pltpu.VMEM((1, 4), bf16),
            pltpu.VMEM((8, KW), bf16),
            pltpu.SMEM((2, 32), jnp.int32),
            pltpu.VMEM((2 * TOK, D // 2), bf16),
            pltpu.VMEM((2 * TOK, KW), bf16),
            pltpu.VMEM((512, KW), bf16),
            pltpu.VMEM((4, 512, KW), bf16),
            pltpu.VMEM((8, 8, YLO, 16, 128), bf16),
            pltpu.VMEM((8, 8, YLO, 16, 128), bf16),
            pltpu.VMEM((2, 2, 4, 4, 2, YLO, 16, 128), bf16),
            pltpu.VMEM((2, 8, YLO, 16, 128), bf16),
            pltpu.VMEM((8, 16, 128), bf16),
            pltpu.VMEM((8, 16, 128), bf16),
            pltpu.VMEM((4, TOK, 512), bf16),
            pltpu.VMEM((4, TOK, 512), bf16),
            dma((9,)), dma((5,)), dma((5,)), dma((2, 3)), dma((2, 3)),
            dma((2, 2, 4, 4)), dma((2, 2, 4, 4)),
            dma((2, 8)), dma((2, 8)), dma((8,)), dma((8,)), dma((4,)), dma((4,)), dma((4,)),
        ],
        compiler_params=pltpu.CompilerParams(
            collective_id=0, has_side_effects=True, vmem_limit_bytes=VMEM_BYTES
        ),
        cost_estimate=pl.CostEstimate(
            flops=4 * TOK * D * KW, bytes_accessed=4 * 1024 * 1024, transcendentals=0
        ),
    )(
        activations, key_grads, w_blocks, w_scales.reshape(1, -1), w_outliers, outlier_rows.T
    )
    return pl.pallas_call(
        hand_on,
        out_shape=shapes,
        in_specs=[hbm] * 2,
        out_specs=(hbm, hbm),
        scratch_shapes=[
            pltpu.VMEM((TOK, D), bf16), pltpu.VMEM((4, KW), jnp.float32), dma((9,)), dma((9,))
        ],
        compiler_params=pltpu.CompilerParams(vmem_limit_bytes=VMEM_BYTES),
    )(*results)


def solution(mesh):
    both = P(("node", "dp"), None)
    return jax.shard_map(
        on_device,
        mesh=mesh,
        in_specs=(both, both, P("node", None), P("node", None), P("node", None), P()),
        out_specs=(both, both),
        check_vma=False,
    )
```

time: 62.2 us -> 55.2 us (0.89)
  local copies, waits for them, and re-layouts: 6.1 us -> 0 us
  Pallas kernels: 55.1 us -> 54.4 us
    unnamed x14 -> x0, local copies, waits for them, and re-layouts: 6.1 us -> none
    pallas_call x1 -> x2, Pallas kernels: 55.1 us -> 54.4 us  [the longest x1 52.3 us: on_device(): pl.pallas_call(kernel, out_shape=shapes, in_specs=[hbm] * 6, out_specs=(h...]
where the time goes in v2:
time: 55.2 us; the launch traced here: 55 us
  Pallas kernels  54.4 us (99%)
  between operations  0.64 us (1%)
    pallas_call x1, Pallas kernels, on_device(): pl.pallas_call(kernel, out_shape=shapes, in_specs=[hbm] * 6, out_specs=(h...  52.3 us
    pallas_call x1, Pallas kernels, on_device(): pl.pallas_call(hand_on, out_shape=shapes, in_specs=[hbm] * 2, out_specs=(...  2.12 us

profile of v2, /device:TPU:2, one launch (start us, length us, event | category | flops | bytes accessed | tf_op | source)
XLA Modules:
  0.0 55.0 jit_solution(11347815312450623958)
XLA Ops:
  0.6 52.3 %shard_map.77 = (bf16[128,4096]{1,0:T(8,128)(2,1)}, f32[4,512]{1,0:T(4,128)}) custom-call(bf16[128,4096]{1,0:T(8,128)(2,1)} %act.1, bf16[128,512]{1,0:T(8,128)(2,1)} %key.1, bf16[512,512]{1,0:T(8,128)(2,1)} %wq.1, bf16[1,4]{1,0:T(2,128)(2,1)} %bitcast.3, bf16[8,512]{1,0:T(8,128)(2,1)} %wout_in.1, s32[2,32]{1,0:T(2,128)} %bitcast.2), custom_call_target="tpu_custom_call" | custom-call | flops 1073741824 | bytes 4194304 | tf_op jit(solution)/shard_map/pallas_call | solution.py:298
  52.9 2.1 %shard_map.78 = (bf16[128,4096]{1,0:T(8,128)(2,1)}, f32[4,512]{1,0:T(4,128)}) custom-call(bf16[128,4096]{1,0:T(8,128)(2,1)} %get-tuple-element.4.ig_in, f32[4,512]{1,0:T(4,128)} %get-tuple-element.5.wg_in), custom_call_target="tpu_custom_call" | custom-call | tf_op jit(solution)/shard_map/pallas_call | solution.py:332

commit v3 on v2

--- a/solution.py
+++ b/solution.py
@@ -21,7 +21,7 @@
     ig, wg,
     scales, wout, rows, a_all, k_all, w_raw, w_all, part0, part1, ring_in, s2_in, s3_out, s3_in, ig_own, ig_sib,
     loc_sem, ex_send, ex_recv, w_send, w_recv, ring_send, ring_recv,
-    s2_send, s2_recv, s3_send, s3_recv, ig_loc, ig_send, ig_recv,
+    s2_send, s2_recv, s3_send, s3_recv, ig_loc, ig_send, ig_recv, token,
 ):
     node, dp = lax.axis_index("node"), lax.axis_index("dp")
     core, ylo = node % 2, node // 2
@@ -57,8 +57,8 @@
         )
 
     barrier = pltpu.get_barrier_semaphore()
-    for step in (4, 3, 5, 2, 6, 1, 7):
-        for along in (on_y, on_x, on_z):
+    for step in (1, -1):
+        for along in (on_x, on_y, on_z):
             pl.semaphore_signal(barrier, inc=1, device_id=along(step), device_id_type=MESH)
     pl.semaphore_signal(barrier, inc=1, device_id=sibling, device_id_type=MESH)
 
@@ -79,7 +79,18 @@
     for copy in (*small, local_w, local_k, *local_a):
         copy.start()
 
-    pl.semaphore_wait(barrier, 1 + 3 * (RING - 1))
+    pl.semaphore_wait(barrier, 7)
+
+    def send_token(direction, r):
+        pl.semaphore_signal(
+            token.at[direction, r], inc=1, device_id=on_y(1 - 2 * direction), device_id_type=MESH
+        )
+
+    def take_token(direction, r):
+        pl.semaphore_wait(token.at[direction, r], 1)
+
+    for direction in range(2):
+        send_token(direction, 0)
 
     exchange = [remote(key, k_all.at[pl.ds(TOK, TOK)], ex_send.at[4], ex_recv.at[4], sibling)]
     for b in range(YLO):
@@ -199,13 +210,24 @@
         copy.start()
         grads[slot] = (local, copy)
 
+    def drain(pair):
+        for copy in pair:
+            copy.wait()
+
     input_grads(0, 0)
     round_of(True, 1)
+    for direction in range(2):
+        take_token(direction, 0)
+        send_token(direction, 1)
     round_of(False, 2)
     relay_weight()
     round_of(True, 2)
+    for direction in range(2):
+        take_token(direction, 1)
+    send_token(0, 2)
     round_of(False, 3)
     round_of(True, 3)
+    take_token(0, 2)
 
     second = {}
     for s in order:
@@ -215,6 +237,7 @@
                 ring[p, direction, s, 3].wait_recv()
                 total = total + ring_in[p, direction, s, 3].astype(jnp.float32)
             part[p][place[p], pl.ds(2 * s, 2)] = total.astype(jnp.bfloat16)
+        for p in range(2):
             for slot in (2 * s, 2 * s + 1):
                 step = (slot + 3) % RING
                 if step == 0:
@@ -229,6 +252,9 @@
     for direction, away in ((0, -1), (1, 1)):
         weight[direction, 1].wait_recv()
         input_grads(1 + direction, away)
+
+    for copy in (*exchange, *ring.values()):
+        copy.wait_send()
 
     quads = [[], []]
     for p in range(2):
@@ -254,6 +280,10 @@
     for direction in range(2):
         weight[direction, 2].wait_recv()
     input_grads(3, 2)
+    for copy in (*second.values(), *weight.values()):
+        copy.wait_send()
+    for slot in range(3):
+        drain(grads.pop(slot))
     total = s3_out[y].astype(jnp.float32)
     for step in (1, 7, 2, 6, 3, 5, 4):
         third[step].wait_recv()
@@ -262,30 +292,20 @@
     for c in range(4):
         wg[:, c * 128 : (c + 1) * 128] = total[4 * c : 4 * c + 4]
 
-    for local, copy in grads.values():
-        local.wait()
-        copy.wait()
-    for copy in exchange:
+    for copy in third.values():
         copy.wait_send()
-    for group in (weight, ring, second, third):
-        for copy in group.values():
-            copy.wait_send()
-
-
-def hand_on(ig_in, wg_in, ig, wg, ig_buf, wg_buf, in_sems, out_sems):
-    pieces = [(wg_in, wg_buf, wg)]
+    drain(grads.pop(3))
+
+
+def hand_on(ig_in, wg_in, ig, wg, sems):
+    copies = [pltpu.make_async_copy(wg_in, wg, sems.at[8])]
     for i in range(8):
         piece = pl.ds(i * 16, 16)
-        pieces.append((ig_in.at[piece], ig_buf.at[piece], ig.at[piece]))
-    loads = [pltpu.make_async_copy(p[0], p[1], in_sems.at[i]) for i, p in enumerate(pieces)]
-    stores = [pltpu.make_async_copy(p[1], p[2], out_sems.at[i]) for i, p in enumerate(pieces)]
-    for load in loads:
-        load.start()
-    for load, store in zip(loads, stores):
-        load.wait()
-        store.start()
-    for store in stores:
-        store.wait()
+        copies.append(pltpu.make_async_copy(ig_in.at[piece], ig.at[piece], sems.at[i]))
+    for copy in copies:
+        copy.start()
+    for copy in copies:
+        copy.wait()
 
 
 def on_device(activations, key_grads, w_blocks, w_scales, w_outliers, outlier_rows):
@@ -297,7 +317,7 @@
     )
     results = pl.pallas_call(
         kernel,
-        out_shape=shapes,
+        out_shape=tuple(pltpu.VMEM(shape.shape, shape.dtype) for shape in shapes),
         in_specs=[hbm] * 6,
         out_specs=(hbm, vmem),
         scratch_shapes=[
@@ -319,6 +339,7 @@
             dma((9,)), dma((5,)), dma((5,)), dma((2, 3)), dma((2, 3)),
             dma((2, 2, 4, 4)), dma((2, 2, 4, 4)),
             dma((2, 8)), dma((2, 8)), dma((8,)), dma((8,)), dma((4,)), dma((4,)), dma((4,)),
+            pltpu.SemaphoreType.REGULAR((2, 3)),
         ],
         compiler_params=pltpu.CompilerParams(
             collective_id=0, has_side_effects=True, vmem_limit_bytes=VMEM_BYTES
@@ -332,12 +353,10 @@
     return pl.pallas_call(
         hand_on,
         out_shape=shapes,
-        in_specs=[hbm] * 2,
+        in_specs=[vmem, vmem],
         out_specs=(hbm, hbm),
-        scratch_shapes=[
-            pltpu.VMEM((TOK, D), bf16), pltpu.VMEM((4, KW), jnp.float32), dma((9,)), dma((9,))
-        ],
-        compiler_params=pltpu.CompilerParams(vmem_limit_bytes=VMEM_BYTES),
+        scratch_shapes=[dma((9,))],
+        compiler_params=pltpu.CompilerParams(vmem_limit_bytes=16 * 1024 * 1024),
     )(*results)
 
 

time: 55.2 us -> 50.8 us (0.920)
  Pallas kernels: 54.4 us -> 50 us
    pallas_call x2, Pallas kernels: 54.4 us -> 50 us  [the longest x1 49 us: on_device(): pl.pallas_call(kernel, out_shape=tuple((pltpu.VMEM(shape.shape, shape.dty...]
where the time goes in v3:
time: 50.8 us; the launch traced here: 50.7 us
  Pallas kernels  50 us (98%)
  between operations  0.64 us (1%)
    pallas_call x1, Pallas kernels, on_device(): pl.pallas_call(kernel, out_shape=tuple((pltpu.VMEM(shape.shape, shape.dty...  49 us
    pallas_call x1, Pallas kernels, on_device(): pl.pallas_call(hand_on, out_shape=shapes, in_specs=[vmem, vmem], out_spec...  1.04 us

profile of v3, /device:TPU:2, one launch (start us, length us, event | category | flops | bytes accessed | tf_op | source)
XLA Modules:
  0.0 50.7 jit_solution(4188092592814120661)
XLA Ops:
  0.6 49.0 %shard_map.77 = (bf16[128,4096]{1,0:T(8,128)(2,1)S(1)}, f32[4,512]{1,0:T(4,128)S(1)}) custom-call(bf16[128,4096]{1,0:T(8,128)(2,1)} %act.1, bf16[128,512]{1,0:T(8,128)(2,1)} %key.1, bf16[512,512]{1,0:T(8,128)(2,1)} %wq.1, bf16[1,4]{1,0:T(2,128)(2,1)} %bitcast.3, bf16[8,512]{1,0:T(8,128)(2,1)} %wout_in.1, s32[2,32]{1,0:T(2,128)} %bitcast.2), custom_call_target="tpu_custom_call" | custom-call | flops 1073741824 | bytes 4194304 | tf_op jit(solution)/shard_map/pallas_call | solution.py:318
  49.6 1.0 %shard_map.78 = (bf16[128,4096]{1,0:T(8,128)(2,1)}, f32[4,512]{1,0:T(4,128)}) custom-call(bf16[128,4096]{1,0:T(8,128)(2,1)S(1)} %get-tuple-element.4.ig_in, f32[4,512]{1,0:T(4,128)S(1)} %get-tuple-element.5.wg_in), custom_call_target="tpu_custom_call" | custom-call | tf_op jit(solution)/shard_map/pallas_call | solution.py:353

commit v4 on v3

--- a/solution.py
+++ b/solution.py
@@ -230,24 +230,34 @@
     take_token(0, 2)
 
     second = {}
-    for s in order:
+
+    def finish_ring(p, s):
+        total = part[p][place[p], pl.ds(2 * s, 2)].astype(jnp.float32)
+        for direction in range(2):
+            ring[p, direction, s, 3].wait_recv()
+            total = total + ring_in[p, direction, s, 3].astype(jnp.float32)
+        part[p][place[p], pl.ds(2 * s, 2)] = total.astype(jnp.bfloat16)
+
+    def send_second(p, s):
+        for slot in (2 * s, 2 * s + 1):
+            step = (slot + 3) % RING
+            if step == 0:
+                continue
+            copy = remote(
+                part[p].at[place[p], slot], s2_in.at[p, step],
+                s2_send.at[p, step], s2_recv.at[p, step], second_axis[p](step),
+            )
+            copy.start()
+            second[p, step] = copy
+
+    for p in range(2):
+        finish_ring(p, order[0])
+    for p in range(2):
+        send_second(p, order[0])
+    for s in order[1:]:
         for p in range(2):
-            total = part[p][place[p], pl.ds(2 * s, 2)].astype(jnp.float32)
-            for direction in range(2):
-                ring[p, direction, s, 3].wait_recv()
-                total = total + ring_in[p, direction, s, 3].astype(jnp.float32)
-            part[p][place[p], pl.ds(2 * s, 2)] = total.astype(jnp.bfloat16)
-        for p in range(2):
-            for slot in (2 * s, 2 * s + 1):
-                step = (slot + 3) % RING
-                if step == 0:
-                    continue
-                copy = remote(
-                    part[p].at[place[p], slot], s2_in.at[p, step],
-                    s2_send.at[p, step], s2_recv.at[p, step], second_axis[p](step),
-                )
-                copy.start()
-                second[p, step] = copy
+            finish_ring(p, s)
+            send_second(p, s)
 
     for direction, away in ((0, -1), (1, 1)):
         weight[direction, 1].wait_recv()

time: 50.8 us -> 50.9 us (level)
  the two profiles are of different devices: /device:TPU:2 before, /device:TPU:14 now
where the time goes in v4:
time: 50.9 us; the launch traced here: 50.8 us
  Pallas kernels  50.1 us (98%)
  between operations  0.64 us (1%)
    pallas_call x1, Pallas kernels, on_device(): pl.pallas_call(kernel, out_shape=tuple((pltpu.VMEM(shape.shape, shape.dty...  49.1 us
    pallas_call x1, Pallas kernels, on_device(): pl.pallas_call(hand_on, out_shape=shapes, in_specs=[vmem, vmem], out_spec...  1.04 us

profile of v4, /device:TPU:14, one launch (start us, length us, event | category | flops | bytes accessed | tf_op | source)
XLA Modules:
  0.0 50.8 jit_solution(17309762660050525552)
XLA Ops:
  0.6 49.1 %shard_map.77 = (bf16[128,4096]{1,0:T(8,128)(2,1)S(1)}, f32[4,512]{1,0:T(4,128)S(1)}) custom-call(bf16[128,4096]{1,0:T(8,128)(2,1)} %act.1, bf16[128,512]{1,0:T(8,128)(2,1)} %key.1, bf16[512,512]{1,0:T(8,128)(2,1)} %wq.1, bf16[1,4]{1,0:T(2,128)(2,1)} %bitcast.3, bf16[8,512]{1,0:T(8,128)(2,1)} %wout_in.1, s32[2,32]{1,0:T(2,128)} %bitcast.2), custom_call_target="tpu_custom_call" | custom-call | flops 1073741824 | bytes 4194304 | tf_op jit(solution)/shard_map/pallas_call | solution.py:328
  49.7 1.0 %shard_map.78 = (bf16[128,4096]{1,0:T(8,128)(2,1)}, f32[4,512]{1,0:T(4,128)}) custom-call(bf16[128,4096]{1,0:T(8,128)(2,1)S(1)} %get-tuple-element.4.ig_in, f32[4,512]{1,0:T(4,128)S(1)} %get-tuple-element.5.wg_in), custom_call_target="tpu_custom_call" | custom-call | tf_op jit(solution)/shard_map/pallas_call | solution.py:363
